TPU v7x, 512 devices: a whole 4x4x16 slice. The times are simulated.
512 devices in a mesh: wide: 16 (over x, z_hi), long: 32 (over z_lo, y, core).
Axes of the slice: x: 4, y: 4, z: 16 (z_hi: 4, z_lo: 4; z = z_hi * 4 + z_lo), core: 2. Of those that a mesh axis runs over, the one named last changes fastest.
Arguments:
- velocity: bfloat16 [3, 128, 1024, 512], P(None, 'wide', 'long'), may hold values from -6 to 6
- vorticity: bfloat16 [3, 128, 1024, 512], P(None, 'wide', 'long'), may hold values from -6 to 6
- m_of_slot: int32 [512], replicated, may hold values from 0 to 511, as said below
- legendre: bfloat16 [512, 512, 512], P('long', 'wide'), as said below
- known_term: bfloat16 [512, 2, 3, 512, 128], P('long', None, None, 'wide'), may hold values from -6 to 6
- inverse: bfloat16 [512, 128, 128], P('wide'), may hold values from -0.5 to 0.5
Outputs:
- section_state: bfloat16 [512, 2, 3, 512, 128], P('long', None, None, 'wide')
Inputs may be any that keep to these rules, and one draw needn't show every extreme that they name: m_of_slot is a permutation of 0 to 511; the m of slot s differs from s by less than 32. legendre[s, l, t] is zero wherever the degree l is below m_of_slot[s].
All inputs are finite; a program needn't handle non-finite values.
Results may differ from a plain program's by a relative error of at most 0.0059.
Values may be sent and summed in bfloat16 or wider, within the bound.
No kernel may reach another device: no remote copies, remote signals or barrier semaphores. Data moves between devices by JAX's collectives and lax.ppermute only.
A program may use at most 192 MiB of HBM per device.

v0:
```python
import math
import jax
import jax.numpy as jnp
from jax import lax
from jax.sharding import PartitionSpec as P

section_step = 0.75


def lamb_product(velocity, vorticity):
    vel = velocity.astype(jnp.float32)
    vort = vorticity.astype(jnp.float32)
    first = vel[1] * vort[2] - vel[2] * vort[1]
    second = vel[2] * vort[0] - vel[0] * vort[2]
    third = vel[0] * vort[1] - vel[1] * vort[0]
    return jnp.stack([first, second, third], axis=0).astype(jnp.bfloat16)


def phase_table(m_of_slot, points):
    column = jnp.arange(points, dtype=jnp.int32)
    paired_modes = jnp.repeat(m_of_slot, 2)
    parity = jnp.arange(paired_modes.shape[0], dtype=jnp.int32) % 2
    product = column[:, None] * paired_modes[None, :] % points
    phase_angle = 2.0 * math.pi / points * product.astype(jnp.float32)
    norm_factor = math.sqrt(2.0 / points)
    values = jnp.where(
        parity[None, :] == 0,
        norm_factor * jnp.cos(phase_angle),
        -norm_factor * jnp.sin(phase_angle),
    )
    return values.astype(jnp.bfloat16)


def body(velocity, vorticity, m_of_slot, legendre, known_term, inverse):
    lamb_vector = lamb_product(velocity, vorticity)
    full_phi = lax.all_to_all(lamb_vector, "long", split_axis=3, concat_axis=2, tiled=True)
    table_local = phase_table(m_of_slot, full_phi.shape[2])
    fourier = jnp.einsum(
        "frjt,jc->frct", full_phi, table_local, preferred_element_type=jnp.float32
    ).astype(jnp.bfloat16)
    slot_major = lax.all_to_all(fourier, "long", split_axis=2, concat_axis=3, tiled=True)
    slot_count = legendre.shape[0]
    nodes = slot_major.shape[3]
    piece = lax.all_gather(slot_major, "wide", axis=1, tiled=True)
    piece_block = piece.reshape(3, piece.shape[1], slot_count, 2, nodes)
    summed = jnp.einsum(
        "frsct,slt->scflr", piece_block, legendre, preferred_element_type=jnp.float32
    )
    coeffs = summed.astype(jnp.bfloat16)
    coeffs = lax.optimization_barrier(coeffs)
    right_side = (
        known_term.astype(jnp.float32) + section_step * coeffs.astype(jnp.float32)
    ).astype(jnp.bfloat16)
    solved = jnp.einsum("scflr,lqr->scflq", right_side, inverse, preferred_element_type=jnp.float32)
    return solved.astype(jnp.bfloat16)


def solution(mesh):
    return jax.shard_map(
        body,
        mesh=mesh,
        in_specs=(
            P(None, "wide", "long", None),
            P(None, "wide", "long", None),
            P(),
            P("long", "wide", None),
            P("long", None, None, "wide", None),
            P("wide", None, None),
        ),
        out_specs=P("long", None, None, "wide", None),
        check_vma=False,
    )
```

profile of v0, /device:TPU:1, one launch (start us, length us, event | category | flops | bytes accessed | tf_op | source)
XLA Modules:
  0.0 1266.5 jit_solution(17308692861983787634)
XLA Ops:
  6.5 0.0 copy-start
  6.5 1.4 convert_element_type.43
  8.0 1.3 convert_element_type.44
  9.3 0.5 subtract_convert_fusion.2
  9.8 0.1 pad_maximum_fusion
  9.9 0.0 copy-start.3
  9.9 3.6 copy.24
  13.5 5.8 reshape.19
  19.3 10.4 all-to-all-start
  29.7 0.2 all-gather.2.cloned.1.call-start
  29.9 0.0 copy-done.3
  30.0 0.1 broadcast_in_dim.14
  30.1 0.2 mul.64
  30.3 21.1 %all-to-all-done = bf16[32,2,6144]{2,1,0:T(2,128)(2,1)S(1)} async-done(((bf16[32,2,6144]{2,1,0:T(2,128)(2,1)}), bf16[32,2,6144]{2,1,0:T(2,128)(2,1)S(1)}, u32[]{:S(2)}, u32[]{:S(2)}) %all-to-all-start) | async-done | bytes 786464 | tf_op jit(solution)/shard_map/all_to_all | solution.py:36
  51.4 2.7 reshape.20
  54.0 5.6 copy.26
  59.6 4.8 all_to_all.29
  64.5 17.9 %fusion.20 = bf16[3,8,1024,16]{2,3,1,0:T(8,128)(2,1)S(1)} fusion(bf16[3,8,1024,16]{2,3,1,0:T(8,128)(2,1)S(1)} %all_to_all.29, s32[1024]{0:T(1024)S(1)} %mul.64, pred[1024]{0:T(1024)(128)(4,1)S(1)} %fusion.28), kind=kOutput, calls=%fused_computation.24 | convolution fusion | flops 824573952 | bytes 1577984 | tf_op jit(solution)/shard_map/frjt,jc->frct/dot_general | solution.py:38
  82.3 6.1 copy.27
  88.4 8.9 reshape.21
  97.3 25.9 %all_to_all.36 = bf16[32,2,6144]{2,1,0:T(2,128)(2,1)S(1)} all-to-all(bf16[32,2,6144]{2,1,0:T(2,128)(2,1)S(1)} %reshape.21), channel_id=1, replica_groups=mesh['wide'=16,'long'=32] {'long'}, dimensions={0} | all-to-all | bytes 1572864 | tf_op jit(solution)/shard_map/all_to_all | solution.py:41
  123.2 5.6 reshape.22
  128.8 7.7 copy.28
  136.5 0.0 all-gather.2.cloned.1.call-update
  136.5 0.0 copy-start.2
  136.5 1068.2 %all-gather.2.cloned.1.call-done = bf16[3,128,32,512]{2,3,1,0:T(8,128)(2,1)} async-done(((bf16[3,8,32,512]{2,3,1,0:T(8,128)(2,1)}), bf16[3,128,32,512]{2,3,1,0:T(8,128)(2,1)}) %all-gather.2.cloned.1.call-update) | async-done | bytes 12582928 | tf_op jit(solution)/shard_map/all_gather | solution.py:44
  1204.7 45.8 %copy.37 = bf16[3,128,32,512]{3,1,0,2:T(8,128)(2,1)} copy(bf16[3,128,32,512]{2,3,1,0:T(8,128)(2,1)} %all-gather.2.cloned.1.call-done) | data formatting | bytes 25165824 | tf_op jit(solution)/shard_map/reshape | solution.py:45
  1250.6 6.8 fusion.24
  1257.4 0.0 copy-done.1
  1257.4 0.3 add_convert_fusion
  1257.7 0.8 fusion.23
  1258.5 1.2 copy.32
  (4 shorter events, 0.0 us)
Async XLA Ops:
  6.5 1251.2 %copy-start = (bf16[32,128,128]{2,1,0:T(8,128)(2,1)S(1)}, bf16[32,128,128]{2,1,0:T(8,128)(2,1)}, u32[]{:S(2)}) copy-start(bf16[32,128,128]{2,1,0:T(8,128)(2,1)} %param.11) | copy-start | bytes 3145732
  9.9 20.1 %copy-start.3 = (s32[512]{0:T(512)S(1)}, s32[512]{0:T(512)}, u32[]{:S(2)}) copy-start(s32[512]{0:T(512)} %param.8) | copy-start | bytes 6148
  19.3 32.1 %all-to-all-start = ((bf16[32,2,6144]{2,1,0:T(2,128)(2,1)}), bf16[32,2,6144]{2,1,0:T(2,128)(2,1)S(1)}, u32[]{:S(2)}, u32[]{:S(2)}) async-start(bf16[32,2,6144]{2,1,0:T(2,128)(2,1)} %reshape.19), calls=%async_computation | async-start | bytes 1572864 | tf_op jit(solution)/shard_map/all_to_all | solution.py:36
  29.7 1175.0 %all-gather.2.cloned.1.call-start = ((), (), s32[]{:S(2)}) async-start(), calls=%async_computation.2 | async-start | bytes 53477376 | tf_op jit(solution)/shard_map/all_gather | solution.py:44
  136.5 1114.0 %copy-start.2 = (bf16[16,32,512]{2,1,0:T(8,128)(2,1)S(1)}, bf16[16,32,512]{2,1,0:T(8,128)(2,1)}, u32[]{:S(2)}) copy-start(bf16[16,32,512]{2,1,0:T(8,128)(2,1)} %param.9) | copy-start | bytes 1572868
  1250.5 6.9 copy-start.1
Sparse Core Ops, SparseCore 0:
  136.6 1068.0 all-gather.1
where the time goes:
time: 1270 us
  waiting for transfers between devices  1090 us (86%)
  local copies, waits for them, and re-layouts  98.1 us (8%)
  blocking collectives  25.9 us (2%)
  matrix products  25.5 us (2%)
  between operations  13.5 us (1%)
    all_gather x1, waiting for transfers between devices, body(): piece = lax.all_gather(slot_major, 'wide', axis=1, tiled=True)  1070 us
    reshape x1, local copies, waits for them, and re-layouts, body(): piece_block = piece.reshape(3, piece.shape[1], slot_count, 2, nodes)  45.8 us
    all_to_all x1, blocking collectives, body(): lax.all_to_all(fourier, 'long', split_axis=2, concat_axis=3, tiled=True)  25.9 us
  transfers between devices with their start and end apart: 2, of which 2 were waited for; matrix products, arithmetic and copies ran while one was open for 0% of the time, Pallas kernels for 0%

commit v1 on v0

--- a/solution.py
+++ b/solution.py
@@ -41,7 +41,9 @@
     slot_major = lax.all_to_all(fourier, "long", split_axis=2, concat_axis=3, tiled=True)
     slot_count = legendre.shape[0]
     nodes = slot_major.shape[3]
-    piece = lax.all_gather(slot_major, "wide", axis=1, tiled=True)
+    piece = jnp.concatenate(
+        lax.all_to_all(jnp.stack([slot_major] * lax.axis_size("wide")), "wide", 0, 0), axis=1
+    )
     piece_block = piece.reshape(3, piece.shape[1], slot_count, 2, nodes)
     summed = jnp.einsum(
         "frsct,slt->scflr", piece_block, legendre, preferred_element_type=jnp.float32

time: 1270 us -> 726 us (0.57)
  waiting for transfers between devices: 1090 us -> 21.3 us
  blocking collectives: 25.9 us -> 589 us
  local copies, waits for them, and re-layouts: 98.1 us -> 67 us
  between operations: 13.5 us -> 0.15 us
    all_gather x1 -> x0, waiting for transfers between devices: 1070 us -> none  [body(): piece = lax.all_gather(slot_major, 'wide', axis=1, tiled=True)]
    all_to_all x0 -> x1, blocking collectives: none -> 563 us  [body(): lax.all_to_all(jnp.stack([slot_major] * lax.axis_size('wide')), 'wide', 0...]
    reshape x1 -> x0, local copies, waits for them, and re-layouts: 45.8 us -> none  [body(): piece_block = piece.reshape(3, piece.shape[1], slot_count, 2, nodes)]
  transfers between devices with their start and end apart: 2 -> 1, of which waited for: 2 -> 1; matrix products, arithmetic and copies ran while one was open for 0% -> 0% of each run, Pallas kernels for 0% -> 0%
where the time goes in v1:
time: 726 us; the launch traced here: 717 us
  blocking collectives  589 us (81%)
  local copies, waits for them, and re-layouts  67 us (9%)
  matrix products  25.5 us (4%)
  waiting for transfers between devices  21.3 us (3%)
  starting transfers between devices  10.5 us (1%)
    all_to_all x1, blocking collectives, body(): lax.all_to_all(jnp.stack([slot_major] * lax.axis_size('wide')), 'wide', 0...  563 us
    all_to_all x1, blocking collectives, body(): lax.all_to_all(fourier, 'long', split_axis=2, concat_axis=3, tiled=True)  25.9 us
    unnamed x12, local copies, waits for them, and re-layouts  23 us
    all_to_all x1, waiting for transfers between devices, body(): lax.all_to_all(lamb_vector, 'long', split_axis=3, concat_axis=2, tiled=True)  21.3 us
    dot_general x1, matrix products, body(): jnp.einsum('frjt,jc->frct', full_phi, table_local, preferred_element_type...  17.9 us
  transfers between devices with their start and end apart: 1, of which 1 were waited for; matrix products, arithmetic and copies ran while one was open for 0% of the time, Pallas kernels for 0%

profile of v1, /device:TPU:1, one launch (start us, length us, event | category | flops | bytes accessed | tf_op | source)
XLA Modules:
  0.0 716.7 jit_solution(11081832800527442826)
XLA Ops:
  0.0 0.0 copy-start
  0.0 1.4 convert_element_type.43
  1.4 1.3 convert_element_type.44
  2.8 0.5 subtract_convert_fusion.2
  3.3 0.1 pad_maximum_fusion
  3.4 0.0 copy-start.2
  3.4 3.6 copy.17
  6.9 5.8 reshape.22
  12.8 10.5 %all-to-all-start = ((bf16[32,2,6144]{2,1,0:T(2,128)(2,1)}), bf16[32,2,6144]{2,1,0:T(2,128)(2,1)S(1)}, u32[]{:S(2)}, u32[]{:S(2)}) async-start(bf16[32,2,6144]{2,1,0:T(2,128)(2,1)} %reshape.22), calls=%async_computation | async-start | bytes 1572864 | tf_op jit(solution)/shard_map/all_to_all | solution.py:36
  23.2 0.0 copy-done.2
  23.2 0.1 broadcast_in_dim.14
  23.3 0.2 mul.64
  23.5 21.3 %all-to-all-done = bf16[32,2,6144]{2,1,0:T(2,128)(2,1)S(1)} async-done(((bf16[32,2,6144]{2,1,0:T(2,128)(2,1)}), bf16[32,2,6144]{2,1,0:T(2,128)(2,1)S(1)}, u32[]{:S(2)}, u32[]{:S(2)}) %all-to-all-start) | async-done | bytes 786464 | tf_op jit(solution)/shard_map/all_to_all | solution.py:36
  44.9 2.7 reshape.23
  47.5 5.6 copy.19
  53.1 4.8 all_to_all.30
  58.0 17.9 %fusion.28 = bf16[3,8,1024,16]{2,3,1,0:T(8,128)(2,1)S(1)} fusion(bf16[3,8,1024,16]{2,3,1,0:T(8,128)(2,1)S(1)} %all_to_all.30, s32[1024]{0:T(1024)S(1)} %mul.64, pred[1024]{0:T(1024)(128)(4,1)S(1)} %fusion.35), kind=kOutput, calls=%fused_computation.27 | convolution fusion | flops 824573952 | bytes 1577984 | tf_op jit(solution)/shard_map/frjt,jc->frct/dot_general | solution.py:38
  75.8 6.1 copy.20
  81.9 8.9 %reshape.24 = bf16[32,2,6144]{2,1,0:T(2,128)(2,1)S(1)} reshape(bf16[1024,3,8,16]{3,2,1,0:T(8,128)(2,1)} %bitcast.44) | data formatting | bytes 1572864
  90.8 25.9 %all_to_all.38 = bf16[32,2,6144]{2,1,0:T(2,128)(2,1)S(1)} all-to-all(bf16[32,2,6144]{2,1,0:T(2,128)(2,1)S(1)} %reshape.24), channel_id=1, replica_groups=mesh['wide'=16,'long'=32] {'long'}, dimensions={0} | all-to-all | bytes 1572864 | tf_op jit(solution)/shard_map/all_to_all | solution.py:41
  116.7 5.6 reshape.25
  122.3 7.7 %copy.21 = bf16[3,8,32,32,16]{3,4,2,1,0:T(8,128)(2,1)} copy(bf16[3,8,32,32,16]{4,1,0,3,2:T(8,128)(2,1)} %bitcast.45) | data formatting | bytes 1572864 | tf_op jit(solution)/shard_map/all_to_all | solution.py:41
  130.0 3.4 copy.22
  133.4 6.0 stack.9
  139.4 562.8 %all_to_all.39 = bf16[16,3,8,32,512]{4,2,3,1,0:T(8,128)(2,1)S(1)} all-to-all(bf16[16,3,8,32,512]{4,2,3,1,0:T(8,128)(2,1)} %stack.9), channel_id=1, replica_groups=mesh['wide'=16,'long'=32] {'wide'}, dimensions={0} | all-to-all | bytes 25165824 | tf_op jit(solution)/shard_map/all_to_all | solution.py:45
  702.2 5.3 copy.23
  707.5 0.0 copy-done.3
  707.6 6.8 fusion.25
  714.4 0.3 add_convert_fusion
  714.7 0.0 copy-done
  714.7 0.8 fusion.31
  715.5 1.2 copy.26
  (4 shorter events, 0.0 us)
Async XLA Ops:
  0.0 714.7 %copy-start = (bf16[32,128,128]{2,1,0:T(8,128)(2,1)S(1)}, bf16[32,128,128]{2,1,0:T(8,128)(2,1)}, u32[]{:S(2)}) copy-start(bf16[32,128,128]{2,1,0:T(8,128)(2,1)} %param.11) | copy-start | bytes 3145732
  3.4 19.8 %copy-start.2 = (s32[512]{0:T(512)S(1)}, s32[512]{0:T(512)}, u32[]{:S(2)}) copy-start(s32[512]{0:T(512)} %param.8) | copy-start | bytes 6148
  12.8 32.1 %all-to-all-start = ((bf16[32,2,6144]{2,1,0:T(2,128)(2,1)}), bf16[32,2,6144]{2,1,0:T(2,128)(2,1)S(1)}, u32[]{:S(2)}, u32[]{:S(2)}) async-start(bf16[32,2,6144]{2,1,0:T(2,128)(2,1)} %reshape.22), calls=%async_computation | async-start | bytes 1572864 | tf_op jit(solution)/shard_map/all_to_all | solution.py:36
  702.2 5.3 copy-start.3
  707.5 6.9 copy-start.1
